TPU v7x, 512 devices: a whole 4x4x16 slice. The times are simulated.
512 devices in a mesh: row: 16 (over z), col: 16 (over x, y), grp: 2 (over core).
Axes of the slice: x: 4, y: 4, z: 16, core: 2. Of those that a mesh axis runs over, the one named last changes fastest.
Arguments:
- grad: bfloat16 [2, 8192, 4096], P('grp', 'row', 'col'), may hold values from -40000 to 40000
- exp_avg: bfloat16 [2, 8192, 4096], P('grp', 'row', 'col'), may hold values from -0.29882812 to 0.29882812
- exp_avg_sq: bfloat16 [2, 8192, 4096], P('grp', 'row', 'col'), may hold values from 0.019897461 to 0.19921875
- left_basis: bfloat16 [2, 8192, 512], P('grp', 'row'), may hold values from -5 to 5
- right_basis: bfloat16 [2, 4096, 256], P('grp', 'col'), may hold values from -5 to 5
- left_stats: float32 [2, 8192, 512], P('grp', 'row', 'col'), may hold values from -0.1 to 0.3, as said below
- right_statistics_blocks: float32 [2, 4096, 256], P('grp', 'col', 'row'), may hold values from -0.1 to 0.3, as said below
Outputs:
- update: bfloat16 [2, 8192, 4096], P('grp', 'row', 'col')
- new_exp_avg: bfloat16 [2, 8192, 4096], P('grp', 'row', 'col')
- new_exp_avg_sq: bfloat16 [2, 8192, 4096], P('grp', 'row', 'col')
- new_left_basis: bfloat16 [2, 8192, 512], P('grp', 'row')
- new_right_basis: bfloat16 [2, 4096, 256], P('grp', 'col')
- new_left_stats: float32 [2, 8192, 512], P('grp', 'row', 'col')
- new_right_stats: float32 [2, 4096, 256], P('grp', 'col', 'row')
Inputs may be any that keep to these rules, and one draw needn't show every extreme that they name: `left_stats`: each of its 512 x 512 blocks is symmetric. `right_statistics_blocks`: each of its 256 x 256 blocks is symmetric.
All inputs are finite; a program needn't handle non-finite values.
Results may differ from a plain program's by a relative error of at most 0.006.
Values may be sent and summed in bfloat16 or wider, within the bound.
A program may use at most 64 MiB of HBM per device.

v0:
```python
import math

import jax
import jax.numpy as jnp
from jax import lax
from jax.sharding import PartitionSpec as P

NS_STEPS = 3


NS_COEFFS = (3.4445, -4.775, 2.0315)
BETA_FIRST = 0.9
BETA_SECOND = 0.99
STATISTICS_DECAY = 0.95
ADAM_EPS = 1e-08
NORM_EPS = 1e-06
MATMUL_PRECISION = lax.Precision.HIGHEST


def gram_of(current):
    return lax.dot_general(current, current, (((0,), (0,)), ((), ())), precision=MATMUL_PRECISION)


def quintic(current, gram_sum):
    inner_poly = NS_COEFFS[1] * gram_sum + NS_COEFFS[2] * jnp.dot(
        gram_sum, gram_sum, precision=MATMUL_PRECISION
    )
    return NS_COEFFS[0] * current + jnp.dot(current, inner_poly, precision=MATMUL_PRECISION)


def orthogonalize(block_panel):
    current = block_panel * lax.rsqrt(jnp.sum(block_panel * block_panel) + NORM_EPS)
    for sweep_index in range(NS_STEPS):
        current = quintic(current, gram_of(current))
    return current


def local(grad, exp_avg, exp_avg_sq, left_basis, right_basis, left_stats, right_statistics_blocks):
    layers = grad.shape[0]
    left_size = grad.shape[1]
    right_size = grad.shape[2]
    col_count = lax.axis_size("col")
    row_count = lax.axis_size("row")
    left_width = left_size // col_count
    right_width = right_size // row_count
    col_index = lax.axis_index("col")
    row_index = lax.axis_index("row")
    total_rows = left_size * row_count
    total_cols = right_size * col_count
    max_norm = math.sqrt(layers * lax.axis_size("grp") * total_rows * total_cols)
    inv_scale = 1.0 / math.sqrt(left_size * right_size)
    left_columns = []
    right_columns = []
    layer_index = 0
    grad_tile = grad[layer_index]
    left_part = lax.dot_general(
        grad_tile, grad_tile, (((1,), (1,)), ((), ())), preferred_element_type=jnp.float32
    )
    right_part = lax.dot_general(
        grad_tile, grad_tile, (((0,), (0,)), ((), ())), preferred_element_type=jnp.float32
    )
    left_full = lax.psum(left_part, "col")
    right_full = lax.psum(right_part, "row")
    full_lefts = [left_full]
    full_rights = [right_full]
    left_columns.append(lax.dynamic_slice_in_dim(left_full, col_index * left_width, left_width, 1))
    right_columns.append(
        lax.dynamic_slice_in_dim(right_full, row_index * right_width, right_width, 1)
    )
    local_sq = jnp.sum(jnp.square(grad.astype(jnp.float32)))
    total_sq = lax.psum(local_sq, ("row", "col", "grp"))
    clip_factor = jnp.minimum(1.0, max_norm * lax.rsqrt(total_sq + NORM_EPS))
    clip_sq = clip_factor * clip_factor
    coef_left = (1.0 - STATISTICS_DECAY) * (clip_sq / total_cols)
    coef_right = (1.0 - STATISTICS_DECAY) * (clip_sq / total_rows)
    layer_index = 0
    grad_tile = grad[layer_index]
    basis_left = left_basis[layer_index]
    basis_right = right_basis[layer_index]
    half_turn = lax.dot_general(
        basis_left, grad_tile, (((0,), (0,)), ((), ())), preferred_element_type=jnp.float32
    ).astype(jnp.bfloat16)
    rotated = jnp.dot(half_turn, basis_right, preferred_element_type=jnp.float32) * (
        clip_factor * inv_scale
    )
    first = BETA_FIRST * exp_avg[layer_index].astype(jnp.float32) + (1.0 - BETA_FIRST) * rotated
    second = (
        BETA_SECOND * exp_avg_sq[layer_index].astype(jnp.float32)
        + (1.0 - BETA_SECOND) * rotated * rotated
    )
    direction = (first / (jnp.sqrt(second) + ADAM_EPS)).astype(jnp.bfloat16)
    back_half = jnp.dot(basis_left, direction, preferred_element_type=jnp.float32).astype(
        jnp.bfloat16
    )
    update = (
        lax.dot_general(
            back_half, basis_right, (((1,), (1,)), ((), ())), preferred_element_type=jnp.float32
        )
        * inv_scale
    )
    updates = [update.astype(jnp.bfloat16)]
    firsts = [first.astype(jnp.bfloat16)]
    seconds = [second.astype(jnp.bfloat16)]
    left_old = lax.all_gather(left_stats[layer_index], "col", axis=1, tiled=True)
    right_old = lax.all_gather(right_statistics_blocks[layer_index], "row", axis=1, tiled=True)
    fresh_left_statistics = STATISTICS_DECAY * left_old + coef_left * full_lefts[layer_index]
    right_new = STATISTICS_DECAY * right_old + coef_right * full_rights[layer_index]
    left_shards = [
        lax.dynamic_slice_in_dim(fresh_left_statistics, col_index * left_width, left_width, 1)
    ]
    right_shards = [lax.dynamic_slice_in_dim(right_new, row_index * right_width, right_width, 1)]
    left_gradient_product = jnp.dot(
        fresh_left_statistics, basis_left.astype(jnp.float32), precision=MATMUL_PRECISION
    )
    right_product = jnp.dot(right_new, basis_right.astype(jnp.float32), precision=MATMUL_PRECISION)
    left_bases = [
        (orthogonalize(left_gradient_product) * math.sqrt(left_size)).astype(jnp.bfloat16)
    ]
    right_bases = [(orthogonalize(right_product) * math.sqrt(right_size)).astype(jnp.bfloat16)]
    return (
        jnp.stack(updates, 0),
        jnp.stack(firsts, 0),
        jnp.stack(seconds, 0),
        jnp.stack(left_bases, 0),
        jnp.stack(right_bases, 0),
        jnp.stack(left_shards, 0),
        jnp.stack(right_shards, 0),
    )


def solution(mesh):
    placed = (
        P("grp", "row", "col"),
        P("grp", "row", "col"),
        P("grp", "row", "col"),
        P("grp", "row", None),
        P("grp", "col", None),
        P("grp", "row", "col"),
        P("grp", "col", "row"),
    )
    return jax.shard_map(
        local,
        mesh=mesh,
        in_specs=placed,
        out_specs=(
            P("grp", "row", "col"),
            P("grp", "row", "col"),
            P("grp", "row", "col"),
            P("grp", "row", None),
            P("grp", "col", None),
            P("grp", "row", "col"),
            P("grp", "col", "row"),
        ),
        check_vma=False,
    )
```

profile of v0, /device:TPU:1, one launch (start us, length us, event | category | flops | bytes accessed | tf_op | source)
XLA Modules:
  0.0 299.9 jit_solution(16408435233115218031)
XLA Ops:
  8.0 0.0 all-reduce.5.cloned.1.call-start
  8.1 2.1 fusion.30
  10.1 0.0 all-reduce.5.cloned.1.call-update
  10.2 0.0 all-gather.4.cloned.1.call-start
  10.2 0.7 copy.20
  10.9 0.0 all-gather.4.cloned.1.call-update
  10.9 0.0 all-reduce.3.cloned.1.call-start
  11.0 0.1 copy-done.1
  11.1 1.3 fusion.32
  12.4 0.7 multiply_reduce_fusion.1
  13.2 112.0 %psum.21 = f32[]{:T(128)} all-reduce(f32[]{:T(128)} %multiply_reduce_fusion.1), channel_id=1, replica_groups=mesh['row'=16,'col'=16,'grp'=2] {'row','col','grp'}, use_global_device_ids=true, to_apply=%region_1.0 | all-reduce | flops 1 | bytes 8 | tf_op jit(solution)/shard_map/psum | solution.py:71
  125.9 0.5 convolution_multiply_fusion.4
  126.4 0.4 copy-done.2
  126.8 0.1 copy-done.3
  126.9 1.6 fusion.7
  128.5 1.0 fusion.28
  129.5 0.7 copy-done.6
  130.2 22.1 %all-gather.1 = f32[1,256,256]{1,0,2:T(1,128)S(1)} all-gather(f32[1,256,16]{1,0,2:T(1,128)S(1)} %copy.22), channel_id=3, replica_groups=mesh['row'=16,'col'=16,'grp'=2] {'row'}, dimensions={2}, use_global_device_ids=true | all-gather | bytes 278528 | tf_op jit(solution)/shard_map/all_gather | solution.py:105
  152.3 0.1 copy.23
  152.5 0.0 all-reduce.5.cloned.1.call-done
  152.5 1.0 bitcast_add_fusion.2
  153.5 0.9 multiply_reduce_fusion.2
  154.4 0.1 constant_dynamic-slice_fusion
  154.5 0.7 copy.25
  155.8 0.6 fusion.46
  156.4 0.4 fusion.11
  156.8 0.4 convolution_add_fusion.5
  157.2 0.6 fusion.67
  157.8 0.4 fusion.10
  158.2 0.4 convolution_add_fusion.4
  158.6 0.6 fusion.68
  159.2 0.4 fusion.9
  159.6 1.0 fusion.13
  160.6 2.5 copy.21
  163.2 106.3 %all-reduce.3.cloned.1.call-done = f32[512,512]{1,0:T(8,128)} async-done(((f32[512,512]{1,0:T(8,128)}), f32[512,512]{1,0:T(8,128)}) %all-reduce.3.cloned.1.call-update) | async-done | bytes 1048592 | tf_op jit(solution)/shard_map/psum | solution.py:62
  269.5 1.5 bitcast_add_fusion
  271.0 1.7 multiply_reduce_fusion
  272.7 0.1 constant_dynamic-slice_fusion.1
  272.8 0.7 copy.24
  274.3 1.9 fusion.14
  276.1 1.9 fusion.3
  278.0 1.9 convolution_add_fusion.2
  279.9 1.9 fusion.65
  281.8 1.9 fusion.2
  283.7 1.9 convolution_add_fusion.1
  285.6 2.1 fusion.66
  287.8 1.9 fusion.1
  289.7 2.7 fusion.5
  (13 shorter events, 0.1 us)
Async XLA Ops:
  8.0 117.9 %copy-start = (bf16[1,512,512]{2,1,0:T(8,128)(2,1)S(1)}, bf16[1,512,512]{2,1,0:T(8,128)(2,1)}, u32[]{:S(2)}) copy-start(bf16[1,512,512]{2,1,0:T(8,128)(2,1)} %param.10) | copy-start | bytes 1572868
  8.0 144.5 %all-reduce.5.cloned.1.call-start = ((), (), s32[]{:S(2)}) async-start(), calls=%async_computation.1 | async-start | bytes 524288 | tf_op jit(solution)/shard_map/psum | solution.py:63
  8.1 2.2 copy-start.5
  10.1 0.9 copy-start.1
  10.2 150.5 %all-gather.4.cloned.1.call-start = ((), (), s32[]{:S(2)}) async-start(), calls=%async_computation.2 | async-start | bytes 1114112 | tf_op jit(solution)/shard_map/all_gather | solution.py:104
  10.9 258.6 %all-reduce.3.cloned.1.call-start = ((), (), s32[]{:S(2)}) async-start(), calls=%async_computation | async-start | bytes 2097152 | tf_op jit(solution)/shard_map/psum | solution.py:62
  12.4 113.5 %copy-start.4 = (bf16[1,256,256]{2,1,0:T(8,128)(2,1)S(1)}, bf16[1,256,256]{2,1,0:T(8,128)(2,1)}, u32[]{:S(2)}) copy-start(bf16[1,256,256]{2,1,0:T(8,128)(2,1)} %param.11) | copy-start | bytes 393220
  125.9 1.0 copy-start.2
  125.9 1.0 copy-start.3
  129.5 0.7 copy-start.6
Sparse Core Ops, SparseCore 0:
  11.7 131.6 all-reduce.4
  147.0 122.4 all-reduce.2
Sparse Core Ops, SparseCore 1:
  14.2 61.7 all-gather.3
where the time goes:
time: 301 us; the launch traced here: 300 us
  blocking collectives  134 us (45%)
  waiting for transfers between devices  106 us (35%)
  matrix products  30.9 us (10%)
  between operations  17.8 us (6%)
  local copies, waits for them, and re-layouts  6.36 us (2%)
  other arithmetic  4.15 us (1%)
    psum x1, blocking collectives, local(): total_sq = lax.psum(local_sq, ('row', 'col', 'grp'))  112 us
    psum x1, waiting for transfers between devices, local(): left_full = lax.psum(left_part, 'col')  106 us
    all_gather x1, blocking collectives, local(): lax.all_gather(right_statistics_blocks[layer_index], 'row', axis=1, tiled...  22.1 us
    dot_general x6, matrix products, quintic(): jnp.dot(current, inner_poly, precision=MATMUL_PRECISION)  8.32 us
    dot_general x6, matrix products, gram_of(): lax.dot_general(current, current, (((0,), (0,)), ((), ())), precision=MAT...  7.68 us
    dot_general x6, matrix products, quintic(): jnp.dot(gram_sum, gram_sum, precision=MATMUL_PRECISION)  6.84 us
  transfers between devices with their start and end apart: 3, of which 1 were waited for; matrix products, arithmetic and copies ran while one was open for 5% of the time, Pallas kernels for 0%

commit v1 on v0

v1 whole, which is shorter than its diff:
```python
import functools
import math

import jax
import jax.numpy as jnp
from jax import lax
from jax.experimental import pallas as pl
from jax.experimental.pallas import tpu as pltpu
from jax.sharding import PartitionSpec as P

NS_STEPS = 3
NS_COEFFS = (3.4445, -4.775, 2.0315)
BETA_FIRST = 0.9
BETA_SECOND = 0.99
STATISTICS_DECAY = 0.95
ADAM_EPS = 1e-08
NORM_EPS = 1e-06
F32 = jnp.float32
BF16 = jnp.bfloat16
MESH = pl.DeviceIdType.MESH
NN = (((1,), (0,)), ((), ()))
NT = (((1,), (1,)), ((), ()))
TN = (((0,), (0,)), ((), ()))


def mm(a, b, dims=NN):
    return lax.dot_general(a, b, dims, preferred_element_type=F32)


def halves(x):
    hi = x.astype(BF16)
    return hi, (x - hi.astype(F32)).astype(BF16)


def mm3(a, b, dims=NN):
    return mm(a[0], b[0], dims) + (mm(a[0], b[1], dims) + mm(a[1], b[0], dims))


def exchange_kernel(
    sizes,
    g_ref, m_ref, v_ref, ql_ref, qr_ref, lold_ref, rold_ref,
    upd_ref, first_ref, second_ref, lfull_out, rfull_out, lnew_ref, rnew_ref,
    lpart, rpart, lin, rin, lfull, rfull, sq_out, sq_plane, sq_mid, sq_line, rot, direction,
    sq_sems, l_sems, r_sems, out_sems,
):
    n_row, n_col, n_grp, max_norm = sizes
    left, right = g_ref.shape
    bl, br = left // n_col, right // n_row
    row, col, grp = lax.axis_index("row"), lax.axis_index("col"), lax.axis_index("grp")
    n_plane = n_col * n_grp
    place = col * n_grp + grp

    def plane_peer(q):
        other = lax.rem(place + q, n_plane)
        return {"col": other // n_grp, "grp": lax.rem(other, n_grp)}

    barrier = pltpu.get_barrier_semaphore()

    @pl.loop(1, n_plane)
    def _(q):
        pl.semaphore_signal(barrier, inc=1, device_id=plane_peer(q), device_id_type=MESH)

    @pl.loop(1, n_row)
    def _(d):
        pl.semaphore_signal(barrier, inc=1, device_id={"row": lax.rem(row + d, n_row)}, device_id_type=MESH)

    g = g_ref[...]
    gf = g.astype(F32)
    local_sq = jnp.sum(gf * gf)
    sq_out[...] = jnp.full((1, 128), local_sq, F32)
    lpart[...] = mm(g, g, NT)
    pl.semaphore_wait(barrier, n_plane - 1 + n_row - 1)

    @pl.loop(1, n_plane)
    def _(q):
        pltpu.make_async_remote_copy(
            src_ref=sq_out, dst_ref=sq_plane.at[q - 1], send_sem=sq_sems.at[0], recv_sem=sq_sems.at[1],
            device_id=plane_peer(q), device_id_type=MESH,
        ).start()

    @pl.loop(1, n_col)
    def _(d):
        other = lax.rem(col + d, n_col)
        pltpu.make_async_remote_copy(
            src_ref=lpart.at[pl.ds(pl.multiple_of(other * bl, bl), bl)], dst_ref=lin.at[d - 1],
            send_sem=l_sems.at[0], recv_sem=l_sems.at[1], device_id={"col": other}, device_id_type=MESH,
        ).start()

    rpart[...] = mm(g, g, TN)

    @pl.loop(1, n_row)
    def _(d):
        other = lax.rem(row + d, n_row)
        pltpu.make_async_remote_copy(
            src_ref=rpart.at[pl.ds(pl.multiple_of(other * br, br), br)], dst_ref=rin.at[d - 1],
            send_sem=r_sems.at[0], recv_sem=r_sems.at[1], device_id={"row": other}, device_id_type=MESH,
        ).start()

    for i in range(left // 128):
        rows = slice(i * 128, (i + 1) * 128)
        half_turn = mm(ql_ref[:, rows], g, TN).astype(BF16)
        rot[rows, :] = mm(half_turn, qr_ref[...])

    pltpu.make_async_copy(sq_plane, sq_plane, sq_sems.at[1]).wait()
    sq_mid[...] = sq_out[...] + jnp.sum(sq_plane[...], axis=0)

    @pl.loop(1, n_row)
    def _(d):
        pltpu.make_async_remote_copy(
            src_ref=sq_mid, dst_ref=sq_line.at[d - 1], send_sem=sq_sems.at[2], recv_sem=sq_sems.at[3],
            device_id={"row": lax.rem(row + d, n_row)}, device_id_type=MESH,
        ).start()

    pltpu.make_async_copy(sq_line, sq_line, sq_sems.at[3]).wait()
    total_sq = (sq_mid[...] + jnp.sum(sq_line[...], axis=0))[:, :1]
    clip = jnp.minimum(1.0, max_norm * lax.rsqrt(total_sq + NORM_EPS))
    clip_sq = clip * clip
    coef_left = (1.0 - STATISTICS_DECAY) * (clip_sq / (right * n_col))
    coef_right = (1.0 - STATISTICS_DECAY) * (clip_sq / (left * n_row))

    pltpu.make_async_copy(lin, lin, l_sems.at[1]).wait()
    mine = pl.ds(pl.multiple_of(col * bl, bl), bl)
    lsum = lpart[mine]
    for d in range(n_col - 1):
        lsum = lsum + lin[d]
    lnew = STATISTICS_DECAY * lold_ref[...] + coef_left * lsum
    lfull[mine] = lnew

    @pl.loop(1, n_col)
    def _(d):
        pltpu.make_async_remote_copy(
            src_ref=lfull.at[mine], dst_ref=lfull.at[mine],
            send_sem=l_sems.at[2], recv_sem=l_sems.at[3],
            device_id={"col": lax.rem(col + d, n_col)}, device_id_type=MESH,
        ).start()

    pltpu.make_async_copy(rin, rin, r_sems.at[1]).wait()
    mine_r = pl.ds(pl.multiple_of(row * br, br), br)
    rsum = rpart[mine_r]
    for d in range(n_row - 1):
        rsum = rsum + rin[d]
    rnew = STATISTICS_DECAY * rold_ref[...] + coef_right * rsum
    rfull[mine_r] = rnew

    @pl.loop(1, n_row)
    def _(d):
        pltpu.make_async_remote_copy(
            src_ref=rfull.at[mine_r], dst_ref=rfull.at[mine_r],
            send_sem=r_sems.at[2], recv_sem=r_sems.at[3],
            device_id={"row": lax.rem(row + d, n_row)}, device_id_type=MESH,
        ).start()

    lnew_ref[...] = lnew
    rnew_ref[...] = rnew
    inv_scale = 1.0 / math.sqrt(left * right)
    turn_scale = clip * inv_scale
    for i in range(left // 64):
        rows = slice(i * 64, (i + 1) * 64)
        rotated = rot[rows, :] * turn_scale
        first = BETA_FIRST * m_ref[rows, :].astype(F32) + (1.0 - BETA_FIRST) * rotated
        second = BETA_SECOND * v_ref[rows, :].astype(F32) + (1.0 - BETA_SECOND) * rotated * rotated
        first_ref[rows, :] = first.astype(BF16)
        second_ref[rows, :] = second.astype(BF16)
        direction[rows, :] = (first / (jnp.sqrt(second) + ADAM_EPS)).astype(BF16)
    for i in range(left // 128):
        rows = slice(i * 128, (i + 1) * 128)
        back_half = mm(ql_ref[rows, :], direction[...]).astype(BF16)
        upd_ref[rows, :] = (mm(back_half, qr_ref[...], NT) * inv_scale).astype(BF16)

    rest = lfull.at[pl.ds(0, left - bl)]
    pltpu.make_async_copy(rest, rest, l_sems.at[3]).wait()
    out_l = pltpu.make_async_copy(lfull, lfull_out, out_sems.at[0])
    out_l.start()
    rest_r = rfull.at[pl.ds(0, right - br)]
    pltpu.make_async_copy(rest_r, rest_r, r_sems.at[3]).wait()
    out_r = pltpu.make_async_copy(rfull, rfull_out, out_sems.at[1])
    out_r.start()
    pltpu.make_async_copy(sq_plane, sq_plane, sq_sems.at[0]).wait()
    pltpu.make_async_copy(sq_line, sq_line, sq_sems.at[2]).wait()
    pltpu.make_async_copy(lin, lin, l_sems.at[0]).wait()
    pltpu.make_async_copy(rin, rin, r_sems.at[0]).wait()
    pltpu.make_async_copy(rest, rest, l_sems.at[2]).wait()
    pltpu.make_async_copy(rest_r, rest_r, r_sems.at[2]).wait()
    out_l.wait()
    out_r.wait()


def refresh_kernel(l_ref, r_ref, ql_ref, qr_ref, *refs):
    count = (len(refs) - 5) // 2
    kept_in, (bl_ref, br_ref), kept_out, (xl, xr, sems) = (
        refs[:count], refs[count:count + 2], refs[count + 2:2 * count + 2], refs[2 * count + 2:]
    )
    copies = [
        pltpu.make_async_copy(src, dst, sems.at[k]) for k, (src, dst) in enumerate(zip(kept_in, kept_out))
    ]
    for copy in copies:
        copy.start()

    def start(stats_ref, basis_ref, x_ref):
        hi, lo = halves(stats_ref[...])
        product = mm(hi, basis_ref[...]) + mm(lo, basis_ref[...])
        x_ref[...] = product * lax.rsqrt(jnp.sum(product * product) + NORM_EPS)

    def step(x_ref):
        x = x_ref[...]
        parts = halves(x)
        gram = mm3(parts, parts, NT)
        gram_parts = halves(gram)
        poly = NS_COEFFS[1] * gram + NS_COEFFS[2] * mm3(gram_parts, gram_parts)
        x_ref[...] = NS_COEFFS[0] * x + mm3(halves(poly), parts)

    start(l_ref, ql_ref, xl)
    start(r_ref, qr_ref, xr)

    @pl.loop(0, NS_STEPS)
    def _(_):
        step(xl)
        step(xr)

    bl_ref[...] = (xl[...] * math.sqrt(xl.shape[0])).astype(BF16)
    br_ref[...] = (xr[...] * math.sqrt(xr.shape[0])).astype(BF16)
    for copy in copies:
        copy.wait()


def local(grad, exp_avg, exp_avg_sq, left_basis, right_basis, left_stats, right_stats, sizes):
    n_row, n_col, n_grp, _ = sizes
    args = [x[0] for x in (grad, exp_avg, exp_avg_sq, left_basis, right_basis)]
    args += [left_stats[0].T, right_stats[0].T]
    left, right = args[0].shape
    bl, br = left // n_col, right // n_row
    vmem = pl.BlockSpec(memory_space=pltpu.VMEM)
    anywhere = pl.BlockSpec(memory_space=pl.ANY)
    tile = jax.ShapeDtypeStruct((left, right), BF16)
    shape = jax.ShapeDtypeStruct
    upd, first, second, lfull, rfull, lnew, rnew = pl.pallas_call(
        functools.partial(exchange_kernel, sizes),
        out_shape=[tile, tile, tile, shape((left, left), F32), shape((right, right), F32),
                   shape((bl, left), F32), shape((br, right), F32)],
        in_specs=[vmem] * 7,
        out_specs=[vmem] * 3 + [anywhere] * 2 + [vmem] * 2,
        scratch_shapes=[
            pltpu.VMEM((left, left), F32),
            pltpu.VMEM((right, right), F32),
            pltpu.VMEM((n_col - 1, bl, left), F32),
            pltpu.VMEM((n_row - 1, br, right), F32),
            pltpu.VMEM((left, left), F32),
            pltpu.VMEM((right, right), F32),
            pltpu.VMEM((1, 128), F32),
            pltpu.VMEM((n_col * n_grp - 1, 1, 128), F32),
            pltpu.VMEM((1, 128), F32),
            pltpu.VMEM((n_row - 1, 1, 128), F32),
            pltpu.VMEM((left, right), F32),
            pltpu.VMEM((left, right), BF16),
            pltpu.SemaphoreType.DMA((4,)),
            pltpu.SemaphoreType.DMA((4,)),
            pltpu.SemaphoreType.DMA((4,)),
            pltpu.SemaphoreType.DMA((2,)),
        ],
        compiler_params=pltpu.CompilerParams(
            collective_id=0, has_side_effects=True, vmem_limit_bytes=32 * 1024 * 1024
        ),
        name="exchange",
    )(*args)
    kept = [upd, first, second, lnew, rnew]
    new_left, new_right, upd, first, second, lnew, rnew = pl.pallas_call(
        refresh_kernel,
        out_shape=[shape((left, left), BF16), shape((right, right), BF16)]
        + [shape(x.shape, x.dtype) for x in kept],
        in_specs=[vmem] * 4 + [anywhere] * 5,
        out_specs=[vmem] * 2 + [anywhere] * 5,
        scratch_shapes=[
            pltpu.VMEM((left, left), F32),
            pltpu.VMEM((right, right), F32),
            pltpu.SemaphoreType.DMA((5,)),
        ],
        compiler_params=pltpu.CompilerParams(vmem_limit_bytes=32 * 1024 * 1024),
        name="refresh",
    )(lfull, rfull, args[3], args[4], *kept)
    return tuple(x[None] for x in (upd, first, second, new_left, new_right, lnew.T, rnew.T))


def solution(mesh):
    n_row, n_col, n_grp = mesh.shape["row"], mesh.shape["col"], mesh.shape["grp"]
    tiled = P("grp", "row", "col")
    by_row, by_col = P("grp", "row", None), P("grp", "col", None)
    turned_tiles = P("grp", "col", "row")

    def step(grad, *rest):
        sizes = (n_row, n_col, n_grp, math.sqrt(grad.size))
        return jax.shard_map(
            functools.partial(local, sizes=sizes),
            mesh=mesh,
            in_specs=(tiled, tiled, tiled, by_row, by_col, tiled, turned_tiles),
            out_specs=(tiled, tiled, tiled, by_row, by_col, tiled, turned_tiles),
            check_vma=False,
        )(grad, *rest)

    return step
```

time: 301 us -> 70.6 us (0.23)
  the two profiles are of different devices: /device:TPU:1 before, /device:TPU:24 now
where the time goes in v1:
time: 70.6 us; the launch traced here: 70.2 us
  Pallas kernels  63.2 us (90%)
  local copies, waits for them, and re-layouts  6.35 us (9%)
    pallas_call x1, Pallas kernels, local(): pl.pallas_call(functools.partial(exchange_kernel, sizes), out_shape=[tile...  50.6 us
    pallas_call x1, Pallas kernels, local(): pl.pallas_call(refresh_kernel, out_shape=[shape((left, left), BF16), shap...  12.6 us
    unnamed x18, local copies, waits for them, and re-layouts  6.35 us

profile of v1, /device:TPU:24, one launch (start us, length us, event | category | flops | bytes accessed | tf_op | source)
XLA Modules:
  0.0 70.2 jit_solution(2870743407392611192)
XLA Ops:
  0.6 0.0 copy-start
  0.6 1.0 %copy-done = bf16[1,512,512]{2,1,0:T(8,128)(2,1)S(1)} copy-done((bf16[1,512,512]{2,1,0:T(8,128)(2,1)S(1)}, bf16[1,512,512]{2,1,0:T(8,128)(2,1)}, u32[]{:S(2)}) %copy-start) | copy-done | bytes 524312
  1.7 0.0 copy-start.2
  1.7 0.9 %copy-done.2 = bf16[1,256,256]{2,1,0:T(8,128)(2,1)S(1)} copy-done((bf16[1,256,256]{2,1,0:T(8,128)(2,1)S(1)}, bf16[1,256,256]{2,1,0:T(8,128)(2,1)}, u32[]{:S(2)}) %copy-start.2) | copy-done | bytes 131096
  2.6 0.0 copy-start.4
  2.6 0.9 %copy-done.4 = bf16[1,512,256]{2,1,0:T(8,128)(2,1)S(1)} copy-done((bf16[1,512,256]{2,1,0:T(8,128)(2,1)S(1)}, bf16[1,512,256]{2,1,0:T(8,128)(2,1)}, u32[]{:S(2)}) %copy-start.4) | copy-done | bytes 262168
  3.5 0.0 copy-start.5
  3.5 0.9 %copy-done.5 = bf16[1,512,256]{2,1,0:T(8,128)(2,1)S(1)} copy-done((bf16[1,512,256]{2,1,0:T(8,128)(2,1)S(1)}, bf16[1,512,256]{2,1,0:T(8,128)(2,1)}, u32[]{:S(2)}) %copy-start.5) | copy-done | bytes 262168
  4.5 0.0 copy-start.6
  4.5 0.9 %copy-done.6 = bf16[1,512,256]{2,1,0:T(8,128)(2,1)S(1)} copy-done((bf16[1,512,256]{2,1,0:T(8,128)(2,1)S(1)}, bf16[1,512,256]{2,1,0:T(8,128)(2,1)}, u32[]{:S(2)}) %copy-start.6) | copy-done | bytes 262168
  5.4 0.0 copy-start.7
  5.4 0.8 %copy-done.7 = f32[1,512,32]{1,2,0:T(8,128)S(1)} copy-done((f32[1,512,32]{1,2,0:T(8,128)S(1)}, f32[1,512,32]{1,2,0:T(8,128)}, u32[]{:S(2)}) %copy-start.7) | copy-done | bytes 65560
  6.3 0.0 copy-start.8
  6.3 0.7 %copy-done.8 = f32[1,256,16]{1,2,0:T(8,128)S(1)} copy-done((f32[1,256,16]{1,2,0:T(8,128)S(1)}, f32[1,256,16]{1,2,0:T(8,128)}, u32[]{:S(2)}) %copy-start.8) | copy-done | bytes 16408
  7.0 0.0 copy-start.1
  7.0 0.0 copy-start.3
  7.0 50.6 %exchange.1 = (bf16[512,256]{1,0:T(8,128)(2,1)S(1)}, bf16[512,256]{1,0:T(8,128)(2,1)S(1)}, bf16[512,256]{1,0:T(8,128)(2,1)S(1)}, f32[512,512]{1,0:T(8,128)S(1)},...) custom-call(bf16[512,256]{1,0:T(8,128)(2,1)S(1)} %bitcast.26, ...), custom_call_target="tpu_custom_call" | custom-call | tf_op jit(solution)/shard_map/exchange/pallas_call | solution.py:236
  57.6 0.0 copy-done.1
  57.7 0.0 copy-done.3
  57.7 12.6 %refresh.1 = (bf16[512,512]{1,0:T(8,128)(2,1)}, bf16[256,256]{1,0:T(8,128)(2,1)}, bf16[512,256]{1,0:T(8,128)(2,1)}, bf16[512,256]{1,0:T(8,128)(2,1)}, bf16[512,2...) custom-call(f32[512,512]{1,0:T(8,128)S(1)} %get-tuple-element.21.l_ref, ...), custom_call_target="tpu_custom_call" | custom-call | tf_op jit(solution)/shard_map/refresh/pallas_call | solution.py:266
Async XLA Ops:
  0.6 1.0 %copy-start = (bf16[1,512,512]{2,1,0:T(8,128)(2,1)S(1)}, bf16[1,512,512]{2,1,0:T(8,128)(2,1)}, u32[]{:S(2)}) copy-start(bf16[1,512,512]{2,1,0:T(8,128)(2,1)} %param.10) | copy-start | bytes 1572868
  1.7 0.9 %copy-start.2 = (bf16[1,256,256]{2,1,0:T(8,128)(2,1)S(1)}, bf16[1,256,256]{2,1,0:T(8,128)(2,1)}, u32[]{:S(2)}) copy-start(bf16[1,256,256]{2,1,0:T(8,128)(2,1)} %param.11) | copy-start | bytes 393220
  2.6 0.9 %copy-start.4 = (bf16[1,512,256]{2,1,0:T(8,128)(2,1)S(1)}, bf16[1,512,256]{2,1,0:T(8,128)(2,1)}, u32[]{:S(2)}) copy-start(bf16[1,512,256]{2,1,0:T(8,128)(2,1)} %param.7) | copy-start | bytes 786436
  3.5 0.9 %copy-start.5 = (bf16[1,512,256]{2,1,0:T(8,128)(2,1)S(1)}, bf16[1,512,256]{2,1,0:T(8,128)(2,1)}, u32[]{:S(2)}) copy-start(bf16[1,512,256]{2,1,0:T(8,128)(2,1)} %param.8) | copy-start | bytes 786436
  4.5 0.9 %copy-start.6 = (bf16[1,512,256]{2,1,0:T(8,128)(2,1)S(1)}, bf16[1,512,256]{2,1,0:T(8,128)(2,1)}, u32[]{:S(2)}) copy-start(bf16[1,512,256]{2,1,0:T(8,128)(2,1)} %param.9) | copy-start | bytes 786436
  5.4 0.8 %copy-start.7 = (f32[1,512,32]{1,2,0:T(8,128)S(1)}, f32[1,512,32]{1,2,0:T(8,128)}, u32[]{:S(2)}) copy-start(f32[1,512,32]{1,2,0:T(8,128)} %param.12) | copy-start | bytes 196612
  6.3 0.7 %copy-start.8 = (f32[1,256,16]{1,2,0:T(8,128)S(1)}, f32[1,256,16]{1,2,0:T(8,128)}, u32[]{:S(2)}) copy-start(f32[1,256,16]{1,2,0:T(8,128)} %param.13) | copy-start | bytes 49156
  7.0 50.7 %copy-start.1 = (bf16[1,512,512]{2,1,0:T(8,128)(2,1)S(1)}, bf16[1,512,512]{2,1,0:T(8,128)(2,1)}, u32[]{:S(2)}) copy-start(bf16[1,512,512]{2,1,0:T(8,128)(2,1)} %param.10) | copy-start | bytes 1572868
  7.0 50.7 %copy-start.3 = (bf16[1,256,256]{2,1,0:T(8,128)(2,1)S(1)}, bf16[1,256,256]{2,1,0:T(8,128)(2,1)}, u32[]{:S(2)}) copy-start(bf16[1,256,256]{2,1,0:T(8,128)(2,1)} %param.11) | copy-start | bytes 393220

commit v2 on v1

v2 whole, which is shorter than its diff:
```python
import functools
import math

import jax
import jax.numpy as jnp
from jax import lax
from jax.experimental import pallas as pl
from jax.experimental.pallas import tpu as pltpu
from jax.sharding import PartitionSpec as P

NS_STEPS = 3
NS_COEFFS = (3.4445, -4.775, 2.0315)
BETA_FIRST = 0.9
BETA_SECOND = 0.99
STATISTICS_DECAY = 0.95
ADAM_EPS = 1e-08
NORM_EPS = 1e-06
F32 = jnp.float32
BF16 = jnp.bfloat16
MESH = pl.DeviceIdType.MESH
NN = (((1,), (0,)), ((), ()))
NT = (((1,), (1,)), ((), ()))
TN = (((0,), (0,)), ((), ()))


def mm(a, b, dims=NN):
    return lax.dot_general(a, b, dims, preferred_element_type=F32)


def halves(x):
    hi = x.astype(BF16)
    return hi, (x - hi.astype(F32)).astype(BF16)


def mm3(a, b, dims=NN):
    return mm(a[0], b[0], dims) + (mm(a[0], b[1], dims) + mm(a[1], b[0], dims))


def packed_far(far, block):
    rows = block * block // 128
    lane = lax.broadcasted_iota(jnp.int32, (rows, 128), 1)
    out = far[:rows]
    for k in range(1, 128 // block):
        out = jnp.where(lane >= k * block, far[k * rows:(k + 1) * rows], out)
    return out


def unpacked_far(packed, block):
    rows = block * block // 128
    lane = lax.broadcasted_iota(jnp.int32, (rows, 128), 1)
    parts = [packed] + [pltpu.roll(packed, 128 - k * block, 1) for k in range(1, 128 // block)]
    return jnp.concatenate([jnp.where(lane < block, part, 0.0) for part in parts], 0)


def step_kernel(
    sizes,
    g_hbm, m_hbm, v_hbm, ql_hbm, qr_hbm, lold_hbm, rold_hbm,
    upd_ref, first_ref, second_ref, newl_ref, newr_ref, lnew_ref, rnew_ref,
    twice, m_ref, v_ref, ql_ref, qr_ref, lold_ref, rold_ref,
    lpart, lin, lgather, lhalf, lfull, rpart, rin, rfull,
    sq_out, sq_line, sq_mid, sq_plane, rot, direction, xl, xr,
    in_sems, sq_sems, l_sems, r_sems,
):
    n_row, n_col, n_grp, max_norm = sizes
    left, right = g_hbm.shape
    bl, br = left // n_col, right // n_row
    far_rows = bl * bl // 128
    row, col, grp = lax.axis_index("row"), lax.axis_index("col"), lax.axis_index("grp")
    n_plane = n_col * n_grp
    place = col * n_grp + grp

    def row_peer(d):
        return {"row": lax.rem(row + d, n_row)}

    def col_peer(d):
        return {"col": lax.rem(col + d, n_col)}

    def plane_peer(q):
        other = lax.rem(place + q, n_plane)
        return {"col": other // n_grp, "grp": lax.rem(other, n_grp)}

    def remote(src, dst, sems, k, peer):
        return pltpu.make_async_remote_copy(
            src_ref=src, dst_ref=dst, send_sem=sems.at[k], recv_sem=sems.at[k + 1],
            device_id=peer, device_id_type=MESH,
        )

    def wait(ref, sem):
        pltpu.make_async_copy(ref, ref, sem).wait()

    fetched = [
        pltpu.make_async_copy(src, dst, in_sems.at[k])
        for k, (src, dst) in enumerate([
            (g_hbm, twice.at[pl.ds(0, left)]), (g_hbm, twice.at[pl.ds(left, left)]),
            (ql_hbm, ql_ref), (qr_hbm, qr_ref), (m_hbm, m_ref), (v_hbm, v_ref),
            (lold_hbm, lold_ref), (rold_hbm, rold_ref),
        ])
    ]
    for copy in fetched:
        copy.start()
    barrier = pltpu.get_barrier_semaphore()

    @pl.loop(1, n_row)
    def _(d):
        pl.semaphore_signal(barrier, inc=1, device_id=row_peer(d), device_id_type=MESH)

    @pl.loop(1, n_plane)
    def _(q):
        pl.semaphore_signal(barrier, inc=1, device_id=plane_peer(q), device_id_type=MESH)

    fetched[0].wait()
    fetched[1].wait()
    g = twice[:left]
    gf = g.astype(F32)
    sq_out[...] = jnp.full((1, 128), jnp.sum(gf * gf), F32)

    @pl.loop(0, n_col)
    def _(t):
        begin = pl.multiple_of(t * bl, bl)
        far = twice[pl.ds(pl.multiple_of(begin + left // 2, bl), bl)]
        others = jnp.concatenate([twice[pl.ds(begin, left // 2)]] + [far] * (128 // bl), 0)
        products = mm(twice[pl.ds(begin, bl)], others, NT)
        for k in range(left // 256):
            lpart[t, k * bl:(k + 1) * bl] = products[:, k * 128:(k + 1) * 128]
        lpart[t, (left // 256) * bl:] = packed_far(products[:, left // 2:], bl)

    rpart[...] = mm(g, g, TN)
    pl.semaphore_wait(barrier, n_plane - 1 + n_row - 1)

    @pl.loop(1, n_row)
    def _(d):
        remote(sq_out, sq_line.at[d - 1], sq_sems, 0, row_peer(d)).start()

    @pl.loop(1, n_col)
    def _(d):
        other = lax.rem(col + d, n_col)
        remote(lpart.at[other], lin.at[d - 1], l_sems, 0, {"col": other}).start()

    @pl.loop(1, n_row)
    def _(d):
        other = lax.rem(row + d, n_row)
        theirs = rpart.at[pl.ds(pl.multiple_of(other * br, br), br)]
        remote(theirs, rin.at[d - 1], r_sems, 0, {"row": other}).start()

    for copy in fetched[2:]:
        copy.wait()
    for i in range(left // 256):
        rows = slice(i * 256, (i + 1) * 256)
        half_turn = mm(ql_ref[:, rows], g, TN).astype(BF16)
        rot[rows, :] = mm(half_turn, qr_ref[...])

    wait(sq_line, sq_sems.at[1])
    sq_mid[...] = sq_out[...] + jnp.sum(sq_line[...], axis=0)

    @pl.loop(1, n_plane)
    def _(q):
        remote(sq_mid, sq_plane.at[q - 1], sq_sems, 2, plane_peer(q)).start()

    lold = pltpu.roll(lold_ref[...], lax.rem(left - col * bl, left), 1)
    lane = lax.broadcasted_iota(jnp.int32, (bl, 128), 1)
    far = jnp.where(lane < bl, lold[:, left // 2:left // 2 + 128], 0.0)
    spread = far
    for k in range(1, 128 // bl):
        spread = spread + pltpu.roll(far, k * bl, 1)
    lold = jnp.concatenate(
        [lold[:, k * 128:(k + 1) * 128] for k in range(left // 256)] + [packed_far(spread, bl)], 0
    )

    wait(sq_plane, sq_sems.at[3])
    total_sq = (sq_mid[...] + jnp.sum(sq_plane[...], axis=0))[:, :1]
    clip = jnp.minimum(1.0, max_norm * lax.rsqrt(total_sq + NORM_EPS))
    clip_sq = clip * clip
    coef_left = (1.0 - STATISTICS_DECAY) * (clip_sq / (right * n_col))
    coef_right = (1.0 - STATISTICS_DECAY) * (clip_sq / (left * n_row))

    wait(lin, l_sems.at[1])
    lsum = lpart[col]
    for d in range(n_col - 1):
        lsum = lsum + lin[d]
    lgather[col] = STATISTICS_DECAY * lold + coef_left * lsum

    @pl.loop(1, n_col)
    def _(d):
        remote(lgather.at[col], lgather.at[col], l_sems, 2, col_peer(d)).start()

    wait(rin, r_sems.at[1])
    mine = pl.ds(pl.multiple_of(row * br, br), br)
    rsum = rpart[mine]
    for d in range(n_row - 1):
        rsum = rsum + rin[d]
    rnew = STATISTICS_DECAY * rold_ref[...] + coef_right * rsum
    rfull[mine] = rnew

    @pl.loop(1, n_row)
    def _(d):
        remote(rfull.at[mine], rfull.at[mine], r_sems, 2, row_peer(d)).start()

    rnew_ref[...] = rnew
    inv_scale = 1.0 / math.sqrt(left * right)
    turn_scale = clip * inv_scale
    for i in range(left // 64):
        rows = slice(i * 64, (i + 1) * 64)
        rotated = rot[rows, :] * turn_scale
        first = BETA_FIRST * m_ref[rows, :].astype(F32) + (1.0 - BETA_FIRST) * rotated
        second = BETA_SECOND * v_ref[rows, :].astype(F32) + (1.0 - BETA_SECOND) * rotated * rotated
        first_ref[rows, :] = first.astype(BF16)
        second_ref[rows, :] = second.astype(BF16)
        direction[rows, :] = (first / (jnp.sqrt(second) + ADAM_EPS)).astype(BF16)
    for i in range(left // 256):
        rows = slice(i * 256, (i + 1) * 256)
        back_half = mm(ql_ref[rows, :], direction[...]).astype(BF16)
        upd_ref[rows, :] = (mm(back_half, qr_ref[...], NT) * inv_scale).astype(BF16)

    wait(lgather.at[pl.ds(0, n_col - 1)], l_sems.at[3])
    for t in range(n_col):
        slab = lgather[t]
        wide = [slab[k * bl:(k + 1) * bl] for k in range(left // 256)]
        wide.append(unpacked_far(slab[(left // 256) * bl:], bl))
        wide.append(jnp.zeros((bl, left // 2 - 128), F32))
        lhalf[t * bl:(t + 1) * bl, :] = pltpu.roll(jnp.concatenate(wide, 1), t * bl, 1)
    shift = bl.bit_length() - 1
    for i in range(left // 128):
        for j in range(left // 128):
            r = lax.broadcasted_iota(jnp.int32, (128, 128), 0) + i * 128
            c = lax.broadcasted_iota(jnp.int32, (128, 128), 1) + j * 128
            held = (((c >> shift) - (r >> shift)) & (n_col - 1)) <= n_col // 2
            here, there = slice(i * 128, (i + 1) * 128), slice(j * 128, (j + 1) * 128)
            lfull[here, there] = jnp.where(held, lhalf[here, there], lhalf[there, here].T)
    lnew_ref[...] = lfull[pl.ds(pl.multiple_of(col * bl, bl), bl)]

    def start(stats_ref, basis_ref, x_ref):
        hi, lo = halves(stats_ref[...])
        product = mm(hi, basis_ref[...]) + mm(lo, basis_ref[...])
        x_ref[...] = product * lax.rsqrt(jnp.sum(product * product) + NORM_EPS)

    def refine(x_ref):
        x = x_ref[...]
        parts = halves(x)
        gram = mm3(parts, parts, NT)
        gram_parts = halves(gram)
        poly = NS_COEFFS[1] * gram + NS_COEFFS[2] * mm3(gram_parts, gram_parts)
        x_ref[...] = NS_COEFFS[0] * x + mm3(halves(poly), parts)

    start(lfull, ql_ref, xl)
    rest = rfull.at[pl.ds(0, right - br)]
    wait(rest, r_sems.at[3])
    start(rfull, qr_ref, xr)

    @pl.loop(0, NS_STEPS)
    def _(_):
        refine(xl)
        refine(xr)

    newl_ref[...] = (xl[...] * math.sqrt(left)).astype(BF16)
    newr_ref[...] = (xr[...] * math.sqrt(right)).astype(BF16)
    wait(sq_line, sq_sems.at[0])
    wait(sq_plane, sq_sems.at[2])
    wait(lin, l_sems.at[0])
    wait(lgather.at[pl.ds(0, n_col - 1)], l_sems.at[2])
    wait(rin, r_sems.at[0])
    wait(rest, r_sems.at[2])


def finish_kernel(*refs):
    count = (len(refs) - 1) // 2
    copies = [pltpu.make_async_copy(refs[k], refs[count + k], refs[-1].at[k]) for k in range(count)]
    for copy in copies:
        copy.start()
    for copy in copies:
        copy.wait()


def local(grad, exp_avg, exp_avg_sq, left_basis, right_basis, left_stats, right_stats, sizes):
    n_row, n_col, n_grp, _ = sizes
    args = [x[0] for x in (grad, exp_avg, exp_avg_sq, left_basis, right_basis)]
    args += [left_stats[0].T, right_stats[0].T]
    left, right = args[0].shape
    bl, br = left // n_col, right // n_row
    wire = (left // 256) * bl + bl * bl // 128
    in_hbm = pl.BlockSpec(memory_space=pltpu.HBM)
    in_vmem = pl.BlockSpec(memory_space=pltpu.VMEM)
    outs = [((left, right), BF16)] * 3 + [
        ((left, left), BF16), ((right, right), BF16), ((bl, left), F32), ((br, right), F32)
    ]
    results = pl.pallas_call(
        functools.partial(step_kernel, sizes),
        out_shape=[pltpu.VMEM(shape, dtype) for shape, dtype in outs],
        in_specs=[in_hbm] * len(args),
        out_specs=[in_vmem] * len(outs),
        scratch_shapes=[
            pltpu.VMEM((2 * left, right), BF16),
            *[pltpu.VMEM(x.shape, x.dtype) for x in args[1:]],
            pltpu.VMEM((n_col, wire, 128), F32),
            pltpu.VMEM((n_col - 1, wire, 128), F32),
            pltpu.VMEM((n_col, wire, 128), F32),
            pltpu.VMEM((left, left), F32),
            pltpu.VMEM((left, left), F32),
            pltpu.VMEM((right, right), F32),
            pltpu.VMEM((n_row - 1, br, right), F32),
            pltpu.VMEM((right, right), F32),
            pltpu.VMEM((1, 128), F32),
            pltpu.VMEM((n_row - 1, 1, 128), F32),
            pltpu.VMEM((1, 128), F32),
            pltpu.VMEM((n_col * n_grp - 1, 1, 128), F32),
            pltpu.VMEM((left, right), F32),
            pltpu.VMEM((left, right), BF16),
            pltpu.VMEM((left, left), F32),
            pltpu.VMEM((right, right), F32),
            pltpu.SemaphoreType.DMA((8,)),
            pltpu.SemaphoreType.DMA((4,)),
            pltpu.SemaphoreType.DMA((4,)),
            pltpu.SemaphoreType.DMA((4,)),
        ],
        compiler_params=pltpu.CompilerParams(
            collective_id=0, has_side_effects=True, vmem_limit_bytes=40 * 1024 * 1024
        ),
        name="step",
    )(*[pltpu.with_memory_space_constraint(x, pltpu.HBM) for x in args])
    results = pl.pallas_call(
        finish_kernel,
        out_shape=[pltpu.HBM(shape, dtype) for shape, dtype in outs],
        in_specs=[in_vmem] * len(outs),
        out_specs=[in_hbm] * len(outs),
        scratch_shapes=[pltpu.SemaphoreType.DMA((len(outs),))],
        name="finish",
    )(*[pltpu.with_memory_space_constraint(x, pltpu.VMEM) for x in results])
    results = [*results[:5], results[5].T, results[6].T]
    return tuple(x[None] for x in results)


def solution(mesh):
    n_row, n_col, n_grp = mesh.shape["row"], mesh.shape["col"], mesh.shape["grp"]
    tiled = P("grp", "row", "col")
    by_row, by_col = P("grp", "row", None), P("grp", "col", None)
    turned_tiles = P("grp", "col", "row")

    def step(grad, *rest):
        sizes = (n_row, n_col, n_grp, math.sqrt(grad.size))
        return jax.shard_map(
            functools.partial(local, sizes=sizes),
            mesh=mesh,
            in_specs=(tiled, tiled, tiled, by_row, by_col, tiled, turned_tiles),
            out_specs=(tiled, tiled, tiled, by_row, by_col, tiled, turned_tiles),
            check_vma=False,
        )(grad, *rest)

    return step
```

time: 70.6 us -> 60.2 us (0.85)
  the two profiles are of different devices: /device:TPU:24 before, /device:TPU:14 now
where the time goes in v2:
time: 60.2 us; the launch traced here: 60.1 us
  Pallas kernels  59.5 us (99%)
  between operations  0.64 us (1%)
    pallas_call x1, Pallas kernels, local(): pl.pallas_call(functools.partial(step_kernel, sizes), out_shape=[pltpu.VM...  58.3 us

profile of v2, /device:TPU:14, one launch (start us, length us, event | category | flops | bytes accessed | tf_op | source)
XLA Modules:
  0.0 60.1 jit_solution(9037792145848213797)
XLA Ops:
  0.6 58.3 %step.1 = (bf16[512,256]{1,0:T(8,128)(2,1)S(1)}, bf16[512,256]{1,0:T(8,128)(2,1)S(1)}, bf16[512,256]{1,0:T(8,128)(2,1)S(1)}, bf16[512,512]{1,0:T(8,128)(2,1)S(1)...) custom-call(bf16[512,256]{1,0:T(8,128)(2,1)} %bitcast.23, ...), custom_call_target="tpu_custom_call" | custom-call | tf_op jit(solution)/shard_map/step/pallas_call | solution.py:285
  58.9 1.2 %finish.1 = (bf16[512,256]{1,0:T(8,128)(2,1)}, bf16[512,256]{1,0:T(8,128)(2,1)}, bf16[512,256]{1,0:T(8,128)(2,1)}, bf16[512,512]{1,0:T(8,128)(2,1)}, bf16[256,25...) custom-call(bf16[512,256]{1,0:T(8,128)(2,1)S(1)} %get-tuple-element.21.refs_0_, ...), custom_call_target="tpu_custom_call" | custom-call | tf_op jit(solution)/shard_map/finish/pallas_call | solution.py:319

commit v3 on v2

v3 whole, which is shorter than its diff:
```python
import functools
import math

import jax
import jax.numpy as jnp
from jax import lax
from jax.experimental import pallas as pl
from jax.experimental.pallas import tpu as pltpu
from jax.sharding import PartitionSpec as P

NS_STEPS = 3
NS_COEFFS = (3.4445, -4.775, 2.0315)
BETA_FIRST = 0.9
BETA_SECOND = 0.99
STATISTICS_DECAY = 0.95
ADAM_EPS = 1e-08
NORM_EPS = 1e-06
F32 = jnp.float32
BF16 = jnp.bfloat16
MESH = pl.DeviceIdType.MESH
NN = (((1,), (0,)), ((), ()))
NT = (((1,), (1,)), ((), ()))
TN = (((0,), (0,)), ((), ()))


def mm(a, b, dims=NN):
    return lax.dot_general(a, b, dims, preferred_element_type=F32)


def halves(x):
    hi = x.astype(BF16)
    return hi, (x - hi.astype(F32)).astype(BF16)


def mm3(a, b, dims=NN):
    return mm(a[0], b[0], dims) + (mm(a[0], b[1], dims) + mm(a[1], b[0], dims))


def wire_rows(size, count):
    block = size // count
    return size // 256 * block + block * block // 128


def to_wire(rows, out):
    block, size = rows.shape
    for k in range(size // 256):
        out[k * block:(k + 1) * block] = rows[:, k * 128:(k + 1) * 128]
    fold = block * block // 128
    far = rows[:, size // 2:size // 2 + 128]
    lane = lax.broadcasted_iota(jnp.int32, (fold, 128), 1)
    folded = far[:fold]
    for k in range(1, 128 // block):
        folded = jnp.where(lane >= k * block, pltpu.roll(far[k * fold:(k + 1) * fold], k * block, 1), folded)
    out[size // 256 * block:] = folded


def from_wire(wire, size, block):
    fold = block * block // 128
    folded = wire[size // 256 * block:]
    lane = lax.broadcasted_iota(jnp.int32, (fold, 128), 1)
    far = [folded] + [pltpu.roll(folded, 128 - k * block, 1) for k in range(1, 128 // block)]
    wide = [wire[k * block:(k + 1) * block] for k in range(size // 256)]
    wide.append(jnp.concatenate([jnp.where(lane < block, part, 0.0) for part in far], 0))
    if size > 256:
        wide.append(jnp.zeros((block, size // 2 - 128), F32))
    return jnp.concatenate(wide, 1)


def pack_all(square, wires):
    count = wires.shape[0]
    size = square.shape[0]
    block = size // count
    for t in range(count):
        rows = square[t * block:(t + 1) * block, :]
        to_wire(pltpu.roll(rows, (size - t * block) % size, 1), wires.at[t])


def unpack_all(wires, half, square):
    count = wires.shape[0]
    size = square.shape[0]
    block = size // count
    for t in range(count):
        half[t * block:(t + 1) * block, :] = pltpu.roll(from_wire(wires[t], size, block), t * block, 1)
    shift = block.bit_length() - 1
    for i in range(size // 128):
        for j in range(size // 128):
            r = lax.broadcasted_iota(jnp.int32, (128, 128), 0) + i * 128
            c = lax.broadcasted_iota(jnp.int32, (128, 128), 1) + j * 128
            held = (((c >> shift) - (r >> shift)) & (count - 1)) <= count // 2
            here, there = slice(i * 128, (i + 1) * 128), slice(j * 128, (j + 1) * 128)
            square[here, there] = jnp.where(held, half[here, there], half[there, here].T)


def part(k):
    return slice(k * 256, (k + 1) * 256)


def square_part(hi, lo, i, j):
    if i == j:
        cross = mm(hi[part(i), :], lo[part(i), :], NT)
        return mm(hi[part(i), :], hi[part(i), :], NT) + (cross + cross.T)
    return mm3((hi[part(i), :], lo[part(i), :]), (hi[part(j), :], lo[part(j), :]), NT)


def refine(x, x_hi, x_lo, poly, gram_hi, gram_lo):
    count = x.shape[0] // 256
    upper = [(i, j) for i in range(count) for j in range(i, count)]
    for i in range(count):
        x_hi[part(i), :], x_lo[part(i), :] = halves(x[part(i), :])
    for i, j in upper:
        gram = square_part(x_hi, x_lo, i, j)
        poly[part(i), part(j)] = gram
        gram_hi[part(i), part(j)], gram_lo[part(i), part(j)] = halves(gram)
        if i != j:
            gram_hi[part(j), part(i)], gram_lo[part(j), part(i)] = halves(gram.T)
    for i, j in upper:
        block = NS_COEFFS[1] * poly[part(i), part(j)] + NS_COEFFS[2] * square_part(gram_hi, gram_lo, i, j)
        poly[part(i), part(j)] = block
        if i != j:
            poly[part(j), part(i)] = block.T
    for i in range(count):
        product = mm3(halves(poly[part(i), :]), (x_hi[...], x_lo[...]))
        x[part(i), :] = NS_COEFFS[0] * x[part(i), :] + product


def step_kernel(
    sizes,
    g_hbm, m_hbm, v_hbm, ql_hbm, qr_hbm, lold_hbm, rold_hbm,
    upd_ref, first_ref, second_ref, newl_ref, newr_ref, lnew_ref, rnew_ref,
    g_ref, m_ref, v_ref, ql_ref, qr_ref, lold_ref, rold_ref,
    lpart, lin, lgather, lhalf, lfull, rpart, rin, rgather, rhalf, rfull,
    sq_out, sq_line, sq_mid, sq_plane, rot, direction, xl, xr,
    l_hi, l_lo, l_poly, lg_hi, lg_lo, r_hi, r_lo, r_poly, rg_hi, rg_lo,
    in_sems, sq_sems, l_sems, r_sems,
):
    n_row, n_col, n_grp, max_norm = sizes
    left, right = g_hbm.shape
    bl, br = left // n_col, right // n_row
    row, col, grp = lax.axis_index("row"), lax.axis_index("col"), lax.axis_index("grp")
    n_plane = n_col * n_grp
    place = col * n_grp + grp

    def row_peer(d):
        return {"row": lax.rem(row + d, n_row)}

    def col_peer(d):
        return {"col": lax.rem(col + d, n_col)}

    def plane_peer(q):
        other = lax.rem(place + q, n_plane)
        return {"col": other // n_grp, "grp": lax.rem(other, n_grp)}

    def remote(src, dst, sems, k, peer):
        return pltpu.make_async_remote_copy(
            src_ref=src, dst_ref=dst, send_sem=sems.at[k], recv_sem=sems.at[k + 1],
            device_id=peer, device_id_type=MESH,
        )

    def wait(ref, sem):
        pltpu.make_async_copy(ref, ref, sem).wait()

    fetched = [
        pltpu.make_async_copy(src, dst, in_sems.at[k])
        for k, (src, dst) in enumerate([
            (g_hbm, g_ref), (ql_hbm, ql_ref), (qr_hbm, qr_ref), (m_hbm, m_ref), (v_hbm, v_ref),
            (lold_hbm, lold_ref), (rold_hbm, rold_ref),
        ])
    ]
    for copy in fetched:
        copy.start()
    barrier = pltpu.get_barrier_semaphore()

    @pl.loop(1, n_row)
    def _(d):
        pl.semaphore_signal(barrier, inc=1, device_id=row_peer(d), device_id_type=MESH)

    @pl.loop(1, n_plane)
    def _(q):
        pl.semaphore_signal(barrier, inc=1, device_id=plane_peer(q), device_id_type=MESH)

    fetched[0].wait()
    g = g_ref[...]
    gf = g.astype(F32)
    sq_out[...] = jnp.full((1, 128), jnp.sum(gf * gf), F32)
    lfull[...] = mm(g, g, NT)
    pack_all(lfull, lpart)
    rfull[...] = mm(g, g, TN)
    pack_all(rfull, rpart)
    pl.semaphore_wait(barrier, n_plane - 1 + n_row - 1)

    @pl.loop(1, n_row)
    def _(d):
        remote(sq_out, sq_line.at[d - 1], sq_sems, 0, row_peer(d)).start()

    @pl.loop(1, n_col)
    def _(d):
        other = lax.rem(col + d, n_col)
        remote(lpart.at[other], lin.at[d - 1], l_sems, 0, {"col": other}).start()

    @pl.loop(1, n_row)
    def _(d):
        other = lax.rem(row + d, n_row)
        remote(rpart.at[other], rin.at[d - 1], r_sems, 0, {"row": other}).start()

    wait(sq_line, sq_sems.at[1])
    sq_mid[...] = sq_out[...] + jnp.sum(sq_line[...], axis=0)

    @pl.loop(1, n_plane)
    def _(q):
        remote(sq_mid, sq_plane.at[q - 1], sq_sems, 2, plane_peer(q)).start()

    for copy in fetched[1:]:
        copy.wait()
    for i in range(left // 256):
        rows = part(i)
        half_turn = mm(ql_ref[:, rows], g, TN).astype(BF16)
        rot[rows, :] = mm(half_turn, qr_ref[...])

    to_wire(pltpu.roll(lold_ref[...], lax.rem(left - col * bl, left), 1), lgather.at[col])
    to_wire(pltpu.roll(rold_ref[...], lax.rem(right - row * br, right), 1), rgather.at[row])

    wait(sq_plane, sq_sems.at[3])
    total_sq = (sq_mid[...] + jnp.sum(sq_plane[...], axis=0))[:, :1]
    clip = jnp.minimum(1.0, max_norm * lax.rsqrt(total_sq + NORM_EPS))
    clip_sq = clip * clip
    coef_left = (1.0 - STATISTICS_DECAY) * (clip_sq / (right * n_col))
    coef_right = (1.0 - STATISTICS_DECAY) * (clip_sq / (left * n_row))

    wait(lin, l_sems.at[1])
    lsum = lpart[col]
    for d in range(n_col - 1):
        lsum = lsum + lin[d]
    lgather[col] = STATISTICS_DECAY * lgather[col] + coef_left * lsum

    @pl.loop(1, n_col)
    def _(d):
        remote(lgather.at[col], lgather.at[col], l_sems, 2, col_peer(d)).start()

    wait(rin, r_sems.at[1])
    rsum = rpart[row]
    for d in range(n_row - 1):
        rsum = rsum + rin[d]
    rgather[row] = STATISTICS_DECAY * rgather[row] + coef_right * rsum

    @pl.loop(1, n_row)
    def _(d):
        remote(rgather.at[row], rgather.at[row], r_sems, 2, row_peer(d)).start()

    inv_scale = 1.0 / math.sqrt(left * right)
    turn_scale = clip * inv_scale
    for i in range(left // 64):
        rows = slice(i * 64, (i + 1) * 64)
        rotated = rot[rows, :] * turn_scale
        first = BETA_FIRST * m_ref[rows, :].astype(F32) + (1.0 - BETA_FIRST) * rotated
        second = BETA_SECOND * v_ref[rows, :].astype(F32) + (1.0 - BETA_SECOND) * rotated * rotated
        first_ref[rows, :] = first.astype(BF16)
        second_ref[rows, :] = second.astype(BF16)
        direction[rows, :] = (first / (jnp.sqrt(second) + ADAM_EPS)).astype(BF16)
    for i in range(left // 256):
        rows = part(i)
        back_half = mm(ql_ref[rows, :], direction[...]).astype(BF16)
        upd_ref[rows, :] = (mm(back_half, qr_ref[...], NT) * inv_scale).astype(BF16)

    def start(stats_ref, basis_ref, x_ref):
        hi, lo = halves(stats_ref[...])
        product = mm(hi, basis_ref[...]) + mm(lo, basis_ref[...])
        x_ref[...] = product * lax.rsqrt(jnp.sum(product * product) + NORM_EPS)

    wait(lgather.at[pl.ds(0, n_col - 1)], l_sems.at[3])
    unpack_all(lgather, lhalf, lfull)
    lnew_ref[...] = lfull[pl.ds(pl.multiple_of(col * bl, bl), bl)]
    start(lfull, ql_ref, xl)
    wait(rgather.at[pl.ds(0, n_row - 1)], r_sems.at[3])
    unpack_all(rgather, rhalf, rfull)
    rnew_ref[...] = rfull[pl.ds(pl.multiple_of(row * br, br), br)]
    start(rfull, qr_ref, xr)

    @pl.loop(0, NS_STEPS)
    def _(_):
        refine(xl, l_hi, l_lo, l_poly, lg_hi, lg_lo)
        refine(xr, r_hi, r_lo, r_poly, rg_hi, rg_lo)

    newl_ref[...] = (xl[...] * math.sqrt(left)).astype(BF16)
    newr_ref[...] = (xr[...] * math.sqrt(right)).astype(BF16)
    wait(sq_line, sq_sems.at[0])
    wait(sq_plane, sq_sems.at[2])
    wait(lin, l_sems.at[0])
    wait(lgather.at[pl.ds(0, n_col - 1)], l_sems.at[2])
    wait(rin, r_sems.at[0])
    wait(rgather.at[pl.ds(0, n_row - 1)], r_sems.at[2])


def finish_kernel(*refs):
    count = (len(refs) - 1) // 2
    copies = [pltpu.make_async_copy(refs[k], refs[count + k], refs[-1].at[k]) for k in range(count)]
    for copy in copies:
        copy.start()
    for copy in copies:
        copy.wait()


def local(grad, exp_avg, exp_avg_sq, left_basis, right_basis, left_stats, right_stats, sizes):
    n_row, n_col, n_grp, _ = sizes
    args = [x[0] for x in (grad, exp_avg, exp_avg_sq, left_basis, right_basis)]
    args += [left_stats[0].T, right_stats[0].T]
    left, right = args[0].shape
    bl, br = left // n_col, right // n_row
    l_wire, r_wire = wire_rows(left, n_col), wire_rows(right, n_row)
    in_hbm = pl.BlockSpec(memory_space=pltpu.HBM)
    in_vmem = pl.BlockSpec(memory_space=pltpu.VMEM)
    outs = [((left, right), BF16)] * 3 + [
        ((left, left), BF16), ((right, right), BF16), ((bl, left), F32), ((br, right), F32)
    ]
    results = pl.pallas_call(
        functools.partial(step_kernel, sizes),
        out_shape=[pltpu.VMEM(shape, dtype) for shape, dtype in outs],
        in_specs=[in_hbm] * len(args),
        out_specs=[in_vmem] * len(outs),
        scratch_shapes=[
            *[pltpu.VMEM(x.shape, x.dtype) for x in args],
            pltpu.VMEM((n_col, l_wire, 128), F32),
            pltpu.VMEM((n_col - 1, l_wire, 128), F32),
            pltpu.VMEM((n_col, l_wire, 128), F32),
            pltpu.VMEM((left, left), F32),
            pltpu.VMEM((left, left), F32),
            pltpu.VMEM((n_row, r_wire, 128), F32),
            pltpu.VMEM((n_row - 1, r_wire, 128), F32),
            pltpu.VMEM((n_row, r_wire, 128), F32),
            pltpu.VMEM((right, right), F32),
            pltpu.VMEM((right, right), F32),
            pltpu.VMEM((1, 128), F32),
            pltpu.VMEM((n_row - 1, 1, 128), F32),
            pltpu.VMEM((1, 128), F32),
            pltpu.VMEM((n_col * n_grp - 1, 1, 128), F32),
            pltpu.VMEM((left, right), F32),
            pltpu.VMEM((left, right), BF16),
            pltpu.VMEM((left, left), F32),
            pltpu.VMEM((right, right), F32),
            *[pltpu.VMEM((size, size), dtype) for size in (left, right) for dtype in (BF16, BF16, F32, BF16, BF16)],
            pltpu.SemaphoreType.DMA((7,)),
            pltpu.SemaphoreType.DMA((4,)),
            pltpu.SemaphoreType.DMA((4,)),
            pltpu.SemaphoreType.DMA((4,)),
        ],
        compiler_params=pltpu.CompilerParams(
            collective_id=0, has_side_effects=True, vmem_limit_bytes=40 * 1024 * 1024
        ),
        name="step",
    )(*[pltpu.with_memory_space_constraint(x, pltpu.HBM) for x in args])
    results = pl.pallas_call(
        finish_kernel,
        out_shape=[pltpu.HBM(shape, dtype) for shape, dtype in outs],
        in_specs=[in_vmem] * len(outs),
        out_specs=[in_hbm] * len(outs),
        scratch_shapes=[pltpu.SemaphoreType.DMA((len(outs),))],
        name="finish",
    )(*[pltpu.with_memory_space_constraint(x, pltpu.VMEM) for x in results])
    results = [*results[:5], results[5].T, results[6].T]
    return tuple(x[None] for x in results)


def solution(mesh):
    n_row, n_col, n_grp = mesh.shape["row"], mesh.shape["col"], mesh.shape["grp"]
    tiled = P("grp", "row", "col")
    by_row, by_col = P("grp", "row", None), P("grp", "col", None)
    turned_tiles = P("grp", "col", "row")

    def step(grad, *rest):
        sizes = (n_row, n_col, n_grp, math.sqrt(grad.size))
        return jax.shard_map(
            functools.partial(local, sizes=sizes),
            mesh=mesh,
            in_specs=(tiled, tiled, tiled, by_row, by_col, tiled, turned_tiles),
            out_specs=(tiled, tiled, tiled, by_row, by_col, tiled, turned_tiles),
            check_vma=False,
        )(grad, *rest)

    return step
```

time: 60.2 us -> 53.5 us (0.89)
  the two profiles are of different devices: /device:TPU:14 before, /device:TPU:1 now
where the time goes in v3:
time: 53.5 us; the launch traced here: 53.4 us
  Pallas kernels  52.8 us (99%)
  between operations  0.64 us (1%)
    pallas_call x1, Pallas kernels, local(): pl.pallas_call(functools.partial(step_kernel, sizes), out_shape=[pltpu.VM...  51.6 us
    pallas_call x1, Pallas kernels, local(): pl.pallas_call(finish_kernel, out_shape=[pltpu.HBM(shape, dtype) for shap...  1.17 us

profile of v3, /device:TPU:1, one launch (start us, length us, event | category | flops | bytes accessed | tf_op | source)
XLA Modules:
  0.0 53.4 jit_solution(17733087301841039277)
XLA Ops:
  0.6 51.6 %step.1 = (bf16[512,256]{1,0:T(8,128)(2,1)S(1)}, bf16[512,256]{1,0:T(8,128)(2,1)S(1)}, bf16[512,256]{1,0:T(8,128)(2,1)S(1)}, bf16[512,512]{1,0:T(8,128)(2,1)S(1)...) custom-call(bf16[512,256]{1,0:T(8,128)(2,1)} %bitcast.23, ...), custom_call_target="tpu_custom_call" | custom-call | tf_op jit(solution)/shard_map/step/pallas_call | solution.py:314
  52.2 1.2 %finish.1 = (bf16[512,256]{1,0:T(8,128)(2,1)}, bf16[512,256]{1,0:T(8,128)(2,1)}, bf16[512,256]{1,0:T(8,128)(2,1)}, bf16[512,512]{1,0:T(8,128)(2,1)}, bf16[256,25...) custom-call(bf16[512,256]{1,0:T(8,128)(2,1)S(1)} %get-tuple-element.21.refs_0_, ...), custom_call_target="tpu_custom_call" | custom-call | tf_op jit(solution)/shard_map/finish/pallas_call | solution.py:350

commit v4 on v3

--- a/solution.py
+++ b/solution.py
@@ -107,20 +107,43 @@
     upper = [(i, j) for i in range(count) for j in range(i, count)]
     for i in range(count):
         x_hi[part(i), :], x_lo[part(i), :] = halves(x[part(i), :])
+    yield
     for i, j in upper:
         gram = square_part(x_hi, x_lo, i, j)
         poly[part(i), part(j)] = gram
         gram_hi[part(i), part(j)], gram_lo[part(i), part(j)] = halves(gram)
         if i != j:
             gram_hi[part(j), part(i)], gram_lo[part(j), part(i)] = halves(gram.T)
+        yield
     for i, j in upper:
         block = NS_COEFFS[1] * poly[part(i), part(j)] + NS_COEFFS[2] * square_part(gram_hi, gram_lo, i, j)
         poly[part(i), part(j)] = block
         if i != j:
             poly[part(j), part(i)] = block.T
+        yield
     for i in range(count):
         product = mm3(halves(poly[part(i), :]), (x_hi[...], x_lo[...]))
         x[part(i), :] = NS_COEFFS[0] * x[part(i), :] + product
+        yield
+
+
+def stages(size):
+    count = size // 256
+    return 1 + count * (count + 1) + count
+
+
+def repeated(times, refs):
+    for _ in range(times):
+        yield from refine(*refs)
+
+
+def weave(main, n_main, other, n_other):
+    done = 0
+    for k in range(n_main):
+        next(main)
+        while done < min(n_other, (k + 1) * n_other // (n_main - 1)):
+            next(other)
+            done += 1
 
 
 def step_kernel(
@@ -192,15 +215,15 @@
     def _(d):
         remote(sq_out, sq_line.at[d - 1], sq_sems, 0, row_peer(d)).start()
 
+    @pl.loop(1, n_row)
+    def _(d):
+        other = lax.rem(row + d, n_row)
+        remote(rpart.at[other], rin.at[d - 1], r_sems, 0, {"row": other}).start()
+
     @pl.loop(1, n_col)
     def _(d):
         other = lax.rem(col + d, n_col)
         remote(lpart.at[other], lin.at[d - 1], l_sems, 0, {"col": other}).start()
-
-    @pl.loop(1, n_row)
-    def _(d):
-        other = lax.rem(row + d, n_row)
-        remote(rpart.at[other], rin.at[d - 1], r_sems, 0, {"row": other}).start()
 
     wait(sq_line, sq_sems.at[1])
     sq_mid[...] = sq_out[...] + jnp.sum(sq_line[...], axis=0)
@@ -269,16 +292,18 @@
     wait(lgather.at[pl.ds(0, n_col - 1)], l_sems.at[3])
     unpack_all(lgather, lhalf, lfull)
     lnew_ref[...] = lfull[pl.ds(pl.multiple_of(col * bl, bl), bl)]
+    left_refs = (xl, l_hi, l_lo, l_poly, lg_hi, lg_lo)
+    right_refs = (xr, r_hi, r_lo, r_poly, rg_hi, rg_lo)
+    l_stages, r_stages = stages(left), stages(right)
     start(lfull, ql_ref, xl)
+    for _ in repeated(1, left_refs):
+        pass
     wait(rgather.at[pl.ds(0, n_row - 1)], r_sems.at[3])
     unpack_all(rgather, rhalf, rfull)
     rnew_ref[...] = rfull[pl.ds(pl.multiple_of(row * br, br), br)]
     start(rfull, qr_ref, xr)
-
-    @pl.loop(0, NS_STEPS)
-    def _(_):
-        refine(xl, l_hi, l_lo, l_poly, lg_hi, lg_lo)
-        refine(xr, r_hi, r_lo, r_poly, rg_hi, rg_lo)
+    rest = NS_STEPS - 1
+    weave(repeated(rest, left_refs), rest * l_stages, repeated(NS_STEPS, right_refs), NS_STEPS * r_stages)
 
     newl_ref[...] = (xl[...] * math.sqrt(left)).astype(BF16)
     newr_ref[...] = (xr[...] * math.sqrt(right)).astype(BF16)

time: 53.5 us -> 49.4 us (0.923)
  Pallas kernels: 52.8 us -> 48.6 us
    pallas_call x1, Pallas kernels: 51.6 us -> 47.5 us  [local(): pl.pallas_call(functools.partial(step_kernel, sizes), out_shape=[pltpu.VM...]
where the time goes in v4:
time: 49.4 us; the launch traced here: 49.3 us
  Pallas kernels  48.6 us (98%)
  between operations  0.64 us (1%)
    pallas_call x1, Pallas kernels, local(): pl.pallas_call(functools.partial(step_kernel, sizes), out_shape=[pltpu.VM...  47.5 us
    pallas_call x1, Pallas kernels, local(): pl.pallas_call(finish_kernel, out_shape=[pltpu.HBM(shape, dtype) for shap...  1.17 us

profile of v4, /device:TPU:1, one launch (start us, length us, event | category | flops | bytes accessed | tf_op | source)
XLA Modules:
  0.0 49.3 jit_solution(16776598661748524979)
XLA Ops:
  0.6 47.5 %step.1 = (bf16[512,256]{1,0:T(8,128)(2,1)S(1)}, bf16[512,256]{1,0:T(8,128)(2,1)S(1)}, bf16[512,256]{1,0:T(8,128)(2,1)S(1)}, bf16[512,512]{1,0:T(8,128)(2,1)S(1)...) custom-call(bf16[512,256]{1,0:T(8,128)(2,1)} %bitcast.23, ...), custom_call_target="tpu_custom_call" | custom-call | tf_op jit(solution)/shard_map/step/pallas_call | solution.py:339
  48.1 1.2 %finish.1 = (bf16[512,256]{1,0:T(8,128)(2,1)}, bf16[512,256]{1,0:T(8,128)(2,1)}, bf16[512,256]{1,0:T(8,128)(2,1)}, bf16[512,512]{1,0:T(8,128)(2,1)}, bf16[256,25...) custom-call(bf16[512,256]{1,0:T(8,128)(2,1)S(1)} %get-tuple-element.21.refs_0_, ...), custom_call_target="tpu_custom_call" | custom-call | tf_op jit(solution)/shard_map/finish/pallas_call | solution.py:375

commit v5 on v4

--- a/solution.py
+++ b/solution.py
@@ -34,6 +34,13 @@
 
 def mm3(a, b, dims=NN):
     return mm(a[0], b[0], dims) + (mm(a[0], b[1], dims) + mm(a[1], b[0], dims))
+
+
+def farthest_first(count, width):
+    def hops(d, n):
+        return min(d % n, -d % n)
+
+    return sorted(range(1, count), key=lambda d: -hops(d // width, count // width) - hops(d, width))
 
 
 def wire_rows(size, count):
@@ -163,6 +170,10 @@
     n_plane = n_col * n_grp
     place = col * n_grp + grp
 
+    side = math.isqrt(n_col)
+    row_order = farthest_first(n_row, n_row)
+    col_order = farthest_first(n_col, side) if side * side == n_col else range(1, n_col)
+
     def row_peer(d):
         return {"row": lax.rem(row + d, n_row)}
 
@@ -211,17 +222,14 @@
     pack_all(rfull, rpart)
     pl.semaphore_wait(barrier, n_plane - 1 + n_row - 1)
 
-    @pl.loop(1, n_row)
-    def _(d):
+    for d in row_order:
         remote(sq_out, sq_line.at[d - 1], sq_sems, 0, row_peer(d)).start()
 
-    @pl.loop(1, n_row)
-    def _(d):
+    for d in row_order:
         other = lax.rem(row + d, n_row)
         remote(rpart.at[other], rin.at[d - 1], r_sems, 0, {"row": other}).start()
 
-    @pl.loop(1, n_col)
-    def _(d):
+    for d in col_order:
         other = lax.rem(col + d, n_col)
         remote(lpart.at[other], lin.at[d - 1], l_sems, 0, {"col": other}).start()
 
@@ -255,8 +263,7 @@
         lsum = lsum + lin[d]
     lgather[col] = STATISTICS_DECAY * lgather[col] + coef_left * lsum
 
-    @pl.loop(1, n_col)
-    def _(d):
+    for d in col_order:
         remote(lgather.at[col], lgather.at[col], l_sems, 2, col_peer(d)).start()
 
     wait(rin, r_sems.at[1])
@@ -265,8 +272,7 @@
         rsum = rsum + rin[d]
     rgather[row] = STATISTICS_DECAY * rgather[row] + coef_right * rsum
 
-    @pl.loop(1, n_row)
-    def _(d):
+    for d in row_order:
         remote(rgather.at[row], rgather.at[row], r_sems, 2, row_peer(d)).start()
 
     inv_scale = 1.0 / math.sqrt(left * right)

time: 49.4 us -> 48.6 us (0.984)
  Pallas kernels: 48.6 us -> 47.8 us
    pallas_call x1, Pallas kernels: 47.5 us -> 46.7 us  [local(): pl.pallas_call(functools.partial(step_kernel, sizes), out_shape=[pltpu.VM...]
where the time goes in v5:
time: 48.6 us; the launch traced here: 48.5 us
  Pallas kernels  47.8 us (98%)
  between operations  0.64 us (1%)
    pallas_call x1, Pallas kernels, local(): pl.pallas_call(functools.partial(step_kernel, sizes), out_shape=[pltpu.VM...  46.7 us
    pallas_call x1, Pallas kernels, local(): pl.pallas_call(finish_kernel, out_shape=[pltpu.HBM(shape, dtype) for shap...  1.17 us

profile of v5, /device:TPU:1, one launch (start us, length us, event | category | flops | bytes accessed | tf_op | source)
XLA Modules:
  0.0 48.5 jit_solution(3097525359533019178)
XLA Ops:
  0.6 46.7 %step.1 = (bf16[512,256]{1,0:T(8,128)(2,1)S(1)}, bf16[512,256]{1,0:T(8,128)(2,1)S(1)}, bf16[512,256]{1,0:T(8,128)(2,1)S(1)}, bf16[512,512]{1,0:T(8,128)(2,1)S(1)...) custom-call(bf16[512,256]{1,0:T(8,128)(2,1)} %bitcast.23, ...), custom_call_target="tpu_custom_call" | custom-call | tf_op jit(solution)/shard_map/step/pallas_call | solution.py:345
  47.3 1.2 %finish.1 = (bf16[512,256]{1,0:T(8,128)(2,1)}, bf16[512,256]{1,0:T(8,128)(2,1)}, bf16[512,256]{1,0:T(8,128)(2,1)}, bf16[512,512]{1,0:T(8,128)(2,1)}, bf16[256,25...) custom-call(bf16[512,256]{1,0:T(8,128)(2,1)S(1)} %get-tuple-element.21.refs_0_, ...), custom_call_target="tpu_custom_call" | custom-call | tf_op jit(solution)/shard_map/finish/pallas_call | solution.py:381

commit v6 on v5

--- a/solution.py
+++ b/solution.py
@@ -82,11 +82,13 @@
         to_wire(pltpu.roll(rows, (size - t * block) % size, 1), wires.at[t])
 
 
-def unpack_all(wires, half, square):
+def unpack_all(wires, half, square, arrived=None):
     count = wires.shape[0]
     size = square.shape[0]
     block = size // count
     for t in range(count):
+        if arrived is not None:
+            arrived(t)
         half[t * block:(t + 1) * block, :] = pltpu.roll(from_wire(wires[t], size, block), t * block, 1)
     shift = block.bit_length() - 1
     for i in range(size // 128):
@@ -161,7 +163,7 @@
     lpart, lin, lgather, lhalf, lfull, rpart, rin, rgather, rhalf, rfull,
     sq_out, sq_line, sq_mid, sq_plane, rot, direction, xl, xr,
     l_hi, l_lo, l_poly, lg_hi, lg_lo, r_hi, r_lo, r_poly, rg_hi, rg_lo,
-    in_sems, sq_sems, l_sems, r_sems,
+    in_sems, sq_sems, l_sems, r_sems, lg_sems,
 ):
     n_row, n_col, n_grp, max_norm = sizes
     left, right = g_hbm.shape
@@ -264,7 +266,10 @@
     lgather[col] = STATISTICS_DECAY * lgather[col] + coef_left * lsum
 
     for d in col_order:
-        remote(lgather.at[col], lgather.at[col], l_sems, 2, col_peer(d)).start()
+        pltpu.make_async_remote_copy(
+            src_ref=lgather.at[col], dst_ref=lgather.at[col], send_sem=l_sems.at[2], recv_sem=lg_sems.at[col],
+            device_id=col_peer(d), device_id_type=MESH,
+        ).start()
 
     wait(rin, r_sems.at[1])
     rsum = rpart[row]
@@ -295,8 +300,12 @@
         product = mm(hi, basis_ref[...]) + mm(lo, basis_ref[...])
         x_ref[...] = product * lax.rsqrt(jnp.sum(product * product) + NORM_EPS)
 
-    wait(lgather.at[pl.ds(0, n_col - 1)], l_sems.at[3])
-    unpack_all(lgather, lhalf, lfull)
+    def arrived(t):
+        @pl.when(t != col)
+        def _():
+            wait(lgather.at[t], lg_sems.at[t])
+
+    unpack_all(lgather, lhalf, lfull, arrived)
     lnew_ref[...] = lfull[pl.ds(pl.multiple_of(col * bl, bl), bl)]
     left_refs = (xl, l_hi, l_lo, l_poly, lg_hi, lg_lo)
     right_refs = (xr, r_hi, r_lo, r_poly, rg_hi, rg_lo)
@@ -372,6 +381,7 @@
             pltpu.SemaphoreType.DMA((4,)),
             pltpu.SemaphoreType.DMA((4,)),
             pltpu.SemaphoreType.DMA((4,)),
+            pltpu.SemaphoreType.DMA((n_col,)),
         ],
         compiler_params=pltpu.CompilerParams(
             collective_id=0, has_side_effects=True, vmem_limit_bytes=40 * 1024 * 1024

time: 48.6 us -> 50 us (1.029)
  Pallas kernels: 47.8 us -> 49.2 us
    pallas_call x1, Pallas kernels: 46.7 us -> 48.1 us  [local(): pl.pallas_call(functools.partial(step_kernel, sizes), out_shape=[pltpu.VM...]
where the time goes in v6:
time: 50 us; the launch traced here: 49.9 us
  Pallas kernels  49.2 us (98%)
  between operations  0.64 us (1%)
    pallas_call x1, Pallas kernels, local(): pl.pallas_call(functools.partial(step_kernel, sizes), out_shape=[pltpu.VM...  48.1 us
    pallas_call x1, Pallas kernels, local(): pl.pallas_call(finish_kernel, out_shape=[pltpu.HBM(shape, dtype) for shap...  1.17 us

profile of v6, /device:TPU:1, one launch (start us, length us, event | category | flops | bytes accessed | tf_op | source)
XLA Modules:
  0.0 49.9 jit_solution(17874943765044385879)
XLA Ops:
  0.6 48.1 %step.1 = (bf16[512,256]{1,0:T(8,128)(2,1)S(1)}, bf16[512,256]{1,0:T(8,128)(2,1)S(1)}, bf16[512,256]{1,0:T(8,128)(2,1)S(1)}, bf16[512,512]{1,0:T(8,128)(2,1)S(1)...) custom-call(bf16[512,256]{1,0:T(8,128)(2,1)} %bitcast.23, ...), custom_call_target="tpu_custom_call" | custom-call | tf_op jit(solution)/shard_map/step/pallas_call | solution.py:354
  48.7 1.2 %finish.1 = (bf16[512,256]{1,0:T(8,128)(2,1)}, bf16[512,256]{1,0:T(8,128)(2,1)}, bf16[512,256]{1,0:T(8,128)(2,1)}, bf16[512,512]{1,0:T(8,128)(2,1)}, bf16[256,25...) custom-call(bf16[512,256]{1,0:T(8,128)(2,1)S(1)} %get-tuple-element.21.refs_0_, ...), custom_call_target="tpu_custom_call" | custom-call | tf_op jit(solution)/shard_map/finish/pallas_call | solution.py:391
